TPU v7x, 512 devices: a whole 4x8x8 slice. The times are simulated.
512 devices in a mesh: dp: 16 (over x, z_hi), section: 32 (over y, z_lo, core).
Axes of the slice: x: 4, y: 8, z: 8 (z_hi: 4, z_lo: 2; z = z_hi * 2 + z_lo), core: 2. Of those that a mesh axis runs over, the one named last changes fastest.
Arguments:
- upstream: bfloat16 [32, 3, 768, 6656], P('section', None, 'dp'), may hold values from -6 to 6
- inputs: bfloat16 [32, 3, 768, 128], P('section', None, 'dp'), may hold values from -6 to 6
- in_proj: bfloat16 [32, 6656, 128], P('section', 'dp'), may hold values from -0.078125 to 0.078125
- out_proj: bfloat16 [32, 6656, 128], P('section', 'dp'), may hold values from -0.5 to 0.5
- in_inverse: float32 [32, 128, 128], P('section'), may hold values from -1 to 15, as said below
- out_inverse: float32 [32, 32, 208, 208], P('section', 'dp'), may hold values from -1 to 15, as said below
- lengths: int32 [32, 16, 3], P('section', 'dp'), may hold values from 1 to 48
Outputs:
- passed: bfloat16 [32, 3, 768, 6656], P('section', None, 'dp')
- precond: float32 [32, 6656, 128], P('section', 'dp')
- in_factor: float32 [32, 128, 128], P('section')
- out_factor: float32 [32, 32, 208, 208], P('section', 'dp')
Inputs may be any that keep to these rules, and one draw needn't show every extreme that they name: `in_inverse`: each 128 x 128 matrix is symmetric. `out_inverse`: each 208 x 208 block is symmetric.
All inputs are finite; a program needn't handle non-finite values.
Results may differ from a plain program's by a relative error of at most 0.0039.
Values may be sent and summed in bfloat16 or wider, within the bound.
A program may use at most 64 MiB of HBM per device.

v0:
```python
import jax
import jax.numpy as jnp
from jax import lax
from jax.sharding import PartitionSpec as P


def from_behind(block, axis, distance):
    devices = range(lax.axis_size(axis))
    route = [(i - distance, i) for i in devices if i - distance in devices]
    return lax.ppermute(block, axis, route)


def local(upstream, inputs, in_proj, out_proj, in_inverse, out_inverse, lengths):
    grads = upstream[0]
    values = inputs[0]
    batches, rows, width = grads.shape
    head_width = values.shape[2]
    position = lax.broadcasted_iota(jnp.int32, (batches, rows), 1)
    keep = (position < lengths[0, 0][:, None]).astype(jnp.bfloat16)[:, :, None]
    grads = grads * keep
    values = values * keep
    flat_grads = grads.reshape(batches * rows, width)
    flat_values = values.reshape(batches * rows, head_width)
    columns = flat_grads
    branch = jnp.dot(
        columns,
        lax.all_gather(out_proj[0], "dp", axis=0, tiled=True),
        preferred_element_type=jnp.float32,
    )
    branch = branch.astype(jnp.bfloat16)
    columns = flat_grads
    act_grad = columns.astype(jnp.float32) + jnp.einsum(
        "th,dh->td",
        branch,
        lax.all_gather(in_proj[0], "dp", axis=0, tiled=True),
        preferred_element_type=jnp.float32,
    )
    act_grad = act_grad.astype(jnp.bfloat16).reshape(1, batches, rows, width)
    passed = from_behind(act_grad, "section", -1)
    counted = jnp.sum(lengths[0, 0]).astype(jnp.float32)
    input_gram = jnp.einsum(
        "th,tg->hg", flat_values, flat_values, preferred_element_type=jnp.float32
    )
    total_gram, total_count = lax.psum((input_gram, counted), "dp")
    in_factor = total_gram / total_count
    split_grads = lax.all_to_all(grads, "dp", split_axis=2, concat_axis=1, tiled=True)
    local_width = split_grads.shape[2]
    blocks = out_inverse.shape[1]
    block_size = out_inverse.shape[2]
    stacked = split_grads.reshape(-1, blocks, block_size)
    out_gram = (
        jnp.einsum("tbi,tbj->bij", stacked, stacked, preferred_element_type=jnp.float32)
        / total_count
    )
    columns = flat_grads
    weight_grad = lax.psum_scatter(
        jnp.einsum("td,th->dh", columns, flat_values, preferred_element_type=jnp.float32),
        "dp",
        scatter_dimension=0,
        tiled=True,
    )
    weight_grad = weight_grad / jnp.sqrt(total_count)
    shaped = weight_grad.reshape(blocks, block_size, head_width)
    left = jnp.einsum("bij,bjh->bih", out_inverse[0], shaped, precision=lax.Precision.HIGHEST)
    precond = jnp.dot(
        left.reshape(local_width, head_width), in_inverse[0], precision=lax.Precision.HIGHEST
    )
    return (passed, precond[None], in_factor[None], out_gram[None])


def solution(mesh):
    in_specs = (
        P("section", None, "dp", None),
        P("section", None, "dp", None),
        P("section", "dp", None),
        P("section", "dp", None),
        P("section", None, None),
        P("section", "dp", None, None),
        P("section", "dp", None),
    )
    out_specs = (
        P("section", None, "dp", None),
        P("section", "dp", None),
        P("section", None, None),
        P("section", "dp", None, None),
    )
    return jax.shard_map(local, mesh=mesh, in_specs=in_specs, out_specs=out_specs, check_vma=False)
```

profile of v0, /device:TPU:1, one launch (start us, length us, event | category | flops | bytes accessed | tf_op | source)
XLA Modules:
  0.0 452.1 jit_solution(10911852607934681098)
XLA Ops:
  8.7 0.7 fusion.29
  9.4 1.7 convolution_bitcast_fusion.2
  11.3 4.5 convolution_bitcast_fusion
  15.8 1.5 copy-done.1
  17.3 7.0 %copy.15 = bf16[1,3,48,6656]{2,1,3,0:T(4,128)(2,1)} copy(bf16[1,3,48,6656]{3,2,1,0:T(8,128)(2,1)S(1)} %copy-done.1) | data formatting | bytes 3833856 | tf_op args[0]
  24.3 7.2 %fusion.30 = bf16[6656,3,48]{2,1,0:T(4,128)(2,1)} fusion(bf16[3,48]{1,0:T(4,128)(2,1)S(1)} %fusion.29, bf16[1,3,48,6656]{2,1,3,0:T(4,128)(2,1)} %copy.15), kind=kLoop, calls=%fused_computation.31 | loop fusion | flops 958464 | bytes 3834144
  31.4 14.2 %reshape.67 = bf16[16,2,29952]{2,1,0:T(2,128)(2,1)} reshape(bf16[6656,3,48]{2,1,0:T(4,128)(2,1)} %fusion.30) | data formatting | bytes 3833856
  45.6 13.5 %all-to-all-start = ((bf16[16,2,29952]{2,1,0:T(2,128)(2,1)}), bf16[16,2,29952]{2,1,0:T(2,128)(2,1)}, u32[]{:S(2)}, u32[]{:S(2)}) async-start(bf16[16,2,29952]{2,1,0:T(2,128)(2,1)} %reshape.67), calls=%async_computation.1 | async-start | bytes 3833856 | tf_op jit(solution)/shard_map/all_to_all | solution.py:46
  59.1 1.7 bitcast_multiply_fusion.1
  60.9 41.3 %all-gather.5.cloned.1.call-done = bf16[1,6656,128]{2,1,0:T(8,128)(2,1)} async-done(((bf16[1,416,128]{2,1,0:T(8,128)(2,1)}), bf16[1,6656,128]{2,1,0:T(8,128)(2,1)}) %all-gather.5.cloned.1.call-update) | async-done | bytes 1703952 | tf_op jit(solution)/shard_map/all_gather | solution.py:27
  102.2 68.7 %all-gather.7.cloned.1.call-done = bf16[1,6656,128]{2,1,0:T(8,128)(2,1)} async-done(((bf16[1,416,128]{2,1,0:T(8,128)(2,1)}), bf16[1,6656,128]{2,1,0:T(8,128)(2,1)}) %all-gather.7.cloned.1.call-update) | async-done | bytes 1703952 | tf_op jit(solution)/shard_map/all_gather | solution.py:35
  170.8 4.5 fusion
  175.3 4.1 collective-permute-start
  180.7 50.7 %psum.14 = f32[]{:T(128)} all-reduce(f32[]{:T(128)S(6)} %convert_element_type.31), channel_id=1, replica_groups=mesh['dp'=16,'section'=32] {'dp'}, use_global_device_ids=true, to_apply=%region_2.0 | all-reduce | flops 1 | bytes 8 | tf_op jit(solution)/shard_map/psum | solution.py:44
  232.1 100.5 %all-reduce.2.cloned.1.call-done = f32[128,128]{1,0:T(8,128)} async-done(((f32[128,128]{1,0:T(8,128)}), f32[128,128]{1,0:T(8,128)}) %all-reduce.2.cloned.1.call-update) | async-done | bytes 65552 | tf_op jit(solution)/shard_map/psum | solution.py:44
  332.6 2.1 divide_bitcast_fusion
  334.7 14.5 %reshape.68 = bf16[6656,3,48]{2,1,0:T(4,128)(2,1)} reshape(bf16[16,2,29952]{2,1,0:T(2,128)(2,1)} %all-to-all-done) | data formatting | bytes 3833856
  349.3 10.1 %copy.16 = bf16[3,48,16,416]{3,1,2,0:T(8,128)(2,1)S(1)} copy(bf16[3,48,16,416]{1,0,3,2:T(4,128)(2,1)} %bitcast.56) | data formatting | bytes 3833856 | tf_op jit(solution)/shard_map/all_to_all | solution.py:46
  359.4 2.7 reshape.61
  362.1 4.9 %fusion.16 = f32[1,2,208,208]{3,2,1,0:T(8,128)} fusion(bf16[2304,2,208]{2,1,0:T(2,128)(2,1)} %reshape.61, f32[]{:T(128)} %psum.14), kind=kOutput, calls=%fused_computation.16 | convolution fusion | flops 398807552 | bytes 2263044 | tf_op jit(solution)/shard_map/tbi,tbj->bij/dot_general | solution.py:52
  367.0 73.1 %reduce-scatter.2.cloned.1.call-done = f32[416,128]{1,0:T(8,128)} async-done(((f32[6656,128]{1,0:T(8,128)}), f32[416,128]{1,0:T(8,128)}) %reduce-scatter.2.cloned.1.call-update) | async-done | bytes 213008 | tf_op jit(solution)/shard_map/reduce_scatter | solution.py:56
  440.2 1.0 broadcast_divide_fusion
  441.6 1.0 convolution_bitcast_fusion.1
  442.7 2.9 copy.27
  (20 shorter events, 2.8 us)
Async XLA Ops:
  7.2 433.9 %copy-start = (f32[1,2,208,208]{3,2,1,0:T(8,128)S(1)}, f32[1,2,208,208]{3,2,1,0:T(8,128)}, u32[]{:S(2)}) copy-start(f32[1,2,208,208]{3,2,1,0:T(8,128)} %param.12) | copy-start | bytes 1038340
  7.2 95.0 %all-gather.5.cloned.1.call-start = ((), (), s32[]{:S(2)}) async-start(), calls=%async_computation.4 | async-start | bytes 1810432 | tf_op jit(solution)/shard_map/all_gather | solution.py:27
  7.9 162.9 %all-gather.7.cloned.1.call-start = ((), (), s32[]{:S(2)}) async-start(), calls=%async_computation.5 | async-start | bytes 1810432 | tf_op jit(solution)/shard_map/all_gather | solution.py:35
  8.7 323.9 %all-reduce.2.cloned.1.call-start = ((), (), s32[]{:S(2)}) async-start(), calls=%async_computation.3 | async-start | bytes 131072 | tf_op jit(solution)/shard_map/psum | solution.py:44
  11.2 428.9 %reduce-scatter.2.cloned.1.call-start = ((), (), s32[]{:S(2)}) async-start(), calls=%async_computation.2 | async-start | bytes 3620864 | tf_op jit(solution)/shard_map/reduce_scatter | solution.py:56
  15.7 1.5 copy-start.1
  45.6 289.2 %all-to-all-start = ((bf16[16,2,29952]{2,1,0:T(2,128)(2,1)}), bf16[16,2,29952]{2,1,0:T(2,128)(2,1)}, u32[]{:S(2)}, u32[]{:S(2)}) async-start(bf16[16,2,29952]{2,1,0:T(2,128)(2,1)} %reshape.67), calls=%async_computation.1 | async-start | bytes 3833856 | tf_op jit(solution)/shard_map/all_to_all | solution.py:46
  60.9 118.5 %copy-start.3 = (s32[1,1,3]{2,1,0:T(1,128)S(1)}, s32[1,1,3]{2,1,0:T(1,128)}, u32[]{:S(2)}) copy-start(s32[1,1,3]{2,1,0:T(1,128)} %param.13) | copy-start | bytes 40
  175.3 191.7 %collective-permute-start = (bf16[1,3,48,6656]{3,2,1,0:T(8,128)(2,1)}, bf16[1,3,48,6656]{3,2,1,0:T(8,128)(2,1)}, u32[]{:S(2)}, u32[]{:S(2)}) collective-permute-start(bf16[1,3,48,6656]{3,2,1,0:T(8,128)(2,1)} %bitcast.58), channel_id=1, source_target_pairs={{1,0},{2,1},{3,2},{4,3},{5,4},{6,5},{7,6},{8,7},{9,8},{10,9},{11,1... | collective-permute-start | bytes 5750792 | tf_op jit(solution)/shard_map/ppermute | solution.py:10
  362.1 79.5 %copy-start.2 = (f32[1,128,128]{2,1,0:T(8,128)S(1)}, f32[1,128,128]{2,1,0:T(8,128)}, u32[]{:S(2)}) copy-start(f32[1,128,128]{2,1,0:T(8,128)} %param.11) | copy-start | bytes 196612
Sparse Core Ops, SparseCore 0:
  11.1 91.0 all-gather.4
  105.2 65.5 all-gather.6
  174.3 158.2 all-reduce.1
  337.3 102.8 reduce-scatter.1
where the time goes:
time: 454 us; the launch traced here: 452 us
  waiting for transfers between devices  285 us (63%)
  local copies, waits for them, and re-layouts  53.1 us (12%)
  blocking collectives  50.7 us (11%)
  starting transfers between devices  17.7 us (4%)
  matrix products  17.1 us (4%)
  between operations  15.2 us (3%)
  other arithmetic  13.3 us (3%)
    psum x1, waiting for transfers between devices, local(): total_gram, total_count = lax.psum((input_gram, counted), 'dp')  101 us
    reduce_scatter x1, waiting for transfers between devices, local(): lax.psum_scatter(jnp.einsum('td,th->dh', columns, flat_values, preferred_...  73.1 us
    all_gather x1, waiting for transfers between devices, local(): lax.all_gather(in_proj[0], 'dp', axis=0, tiled=True)  68.7 us
    psum x1, blocking collectives, local(): total_gram, total_count = lax.psum((input_gram, counted), 'dp')  50.7 us
    all_gather x1, waiting for transfers between devices, local(): lax.all_gather(out_proj[0], 'dp', axis=0, tiled=True)  41.3 us
    unnamed x12, local copies, waits for them, and re-layouts  40.1 us
    all_to_all x1, starting transfers between devices, local(): lax.all_to_all(grads, 'dp', split_axis=2, concat_axis=1, tiled=True)  13.5 us
    all_to_all x1, local copies, waits for them, and re-layouts, local(): lax.all_to_all(grads, 'dp', split_axis=2, concat_axis=1, tiled=True)  10.1 us
  transfers between devices with their start and end apart: 6, of which 4 were waited for; matrix products, arithmetic and copies ran while one was open for 17% of the time, Pallas kernels for 0%

commit v1 on v0

v1 whole, which is shorter than its diff:
```python
import functools

import jax
import jax.numpy as jnp
from jax import lax
from jax.experimental import pallas as pl
from jax.experimental.pallas import tpu as pltpu
from jax.sharding import PartitionSpec as P

RING = 4
BF16 = jnp.bfloat16
F32 = jnp.float32


def nt_dot(a, b):
    return lax.dot_general(a, b, (((1,), (1,)), ((), ())), preferred_element_type=F32)


def tn_dot(a, b):
    return lax.dot_general(a, b, (((0,), (0,)), ((), ())), preferred_element_type=F32)


def kernel(
    lengths, upstream, inputs, in_proj, out_proj, in_inverse, out_inverse,
    passed, precond, in_factor, out_factor,
    grads, split, split_t, relayed, values, out_rows, in_rows, partial, partial_in, branch, branch_in,
    stats, stats_in, split_send, split_recv, value_send, value_recv, out_send, out_recv,
    relay_send, relay_recv, in_send, in_recv, partial_send, partial_recv, stats_send, stats_recv,
):
    rows, width = upstream.shape
    slots = rows // lengths.shape[0]
    shard = in_proj.shape[0]
    blocks, size, _ = out_inverse.shape
    head = in_proj.shape[1]
    span = RING * shard
    sections = lax.axis_size("section")
    dp = lax.axis_index("dp")
    section = lax.axis_index("section")
    x = lax.div(dp, RING)
    z = lax.rem(dp, RING)
    before = {"section": lax.rem(section + sections - 1, sections)}
    after = {"section": lax.rem(section + 1, sections)}

    def along_x(r):
        return {"dp": lax.rem(x + r, RING) * RING + z}

    def along_z(r):
        return {"dp": x * RING + lax.rem(z + r, RING)}

    def send(src, dst, send_sem, recv_sem, device):
        copy = pltpu.make_async_remote_copy(
            src_ref=src, dst_ref=dst, send_sem=send_sem, recv_sem=recv_sem,
            device_id=device, device_id_type=pl.DeviceIdType.MESH,
        )
        copy.start()
        return copy

    barrier = pltpu.get_barrier_semaphore()
    for device in [along_x(r) for r in (1, 2, 3)] + [along_z(r) for r in (1, 2, 3)] + [before, after]:
        pl.semaphore_signal(barrier, inc=1, device_id=device, device_id_type=pl.DeviceIdType.MESH)

    position = lax.broadcasted_iota(jnp.int32, (rows, 1), 0)
    batch = lax.div(position, slots)
    limit = jnp.where(batch == 0, lengths[0], jnp.where(batch == 1, lengths[1], lengths[2]))
    keep = (lax.rem(position, slots) < limit).astype(F32)
    keep = jnp.broadcast_to(keep, (rows, head)).astype(BF16)
    counted = (lengths[0] + lengths[1] + lengths[2]).astype(F32)
    values[0, 0:rows, :] = inputs[...] * keep
    values[0, rows:, :] = jnp.full((values.shape[1] - rows, head), counted, F32).astype(BF16)
    own_out = pl.ds(pl.multiple_of(z * shard, 16), shard)
    out_rows[own_out, :] = out_proj[...]

    def mask(first, columns):
        for c in range(columns // head):
            where = pl.ds(pl.multiple_of(first + c * head, head), head)
            grads[:, where] = upstream[:, where] * keep

    pl.semaphore_wait(barrier, 8)

    copies = []
    outs = [send(out_proj, out_rows.at[own_out], out_send.at[r - 1], out_recv.at[r - 1], along_z(r)) for r in (1, 2, 3)]
    vals = [send(values.at[0], values.at[r], value_send.at[r - 1], value_recv.at[r - 1], along_x(r)) for r in (1, 2, 3)]
    own_in = pl.ds(pl.multiple_of(dp * shard, 16), shard)
    ins = send(in_proj, in_rows.at[own_in], in_send.at[0], in_recv.at[0], before)
    splits = {}
    for r in (2, 1, 3):
        first = lax.rem(x + r, RING) * span
        mask(first, span)
        splits[r] = send(
            grads.at[:, pl.ds(pl.multiple_of(first, head), span)], split.at[pl.ds(r * rows, rows)],
            split_send.at[r - 1], split_recv.at[r - 1], along_x(r),
        )
    mask(x * span, span)
    relay = send(grads, relayed, relay_send.at[0], relay_recv.at[0], before)
    for c in range(span // head):
        where = pl.ds(pl.multiple_of(x * span + c * head, head), head)
        split[0:rows, c * head:(c + 1) * head] = grads[:, where]

    ins.wait_recv()
    ins_z = [
        send(in_rows.at[own_in], in_rows.at[own_in], in_send.at[r], in_recv.at[r], along_z(r)) for r in (1, 2, 3)
    ]

    for copy in outs + vals:
        copy.wait_recv()
    for r in (1, 2, 3):
        splits[r].wait_recv()

    part = jnp.dot(split[...], out_rows[...], preferred_element_type=F32)
    partial[...] = part.astype(BF16)
    partials = [
        send(
            partial.at[pl.ds(r * rows, rows)], partial_in.at[r - 1],
            partial_send.at[r - 1], partial_recv.at[r - 1], along_x(RING - r),
        )
        for r in (1, 2, 3)
    ]

    split_t[...] = split[...].T
    stacked = jnp.concatenate([values[r, 0:rows, :] for r in range(RING)], axis=0)
    gram_in = tn_dot(stacked, stacked)
    count_rows = values[0, rows:, :].astype(F32)
    row = lax.broadcasted_iota(jnp.int32, count_rows.shape, 0)
    counts = jnp.zeros_like(count_rows)
    for r in range(RING):
        counts = jnp.where(row == r, values[r, rows:, :].astype(F32), counts)
    packed = size + size - head
    at_weight = blocks * packed
    at_gram = at_weight + shard
    at_count = at_gram + head
    for k in range(RING):
        for b in range(blocks):
            g = split_t[k * shard + b * size:k * shard + (b + 1) * size, :]
            gram = nt_dot(g, g)
            stats[k, b * packed:b * packed + size, :] = gram[:, 0:head].astype(BF16)
            stats[k, b * packed + size:(b + 1) * packed, 0:size - head] = gram[head:, head:].astype(BF16)
        weight = jnp.dot(split_t[k * shard:(k + 1) * shard, :], stacked, preferred_element_type=F32)
        stats[k, at_weight:at_gram, :] = weight.astype(BF16)
        stats[k, at_gram:at_count, :] = gram_in.astype(BF16)
        stats[k, at_count:, :] = counts.astype(BF16)
    stat = [
        send(
            stats.at[lax.rem(z + r, RING)], stats_in.at[r - 1],
            stats_send.at[r - 1], stats_recv.at[r - 1], along_z(r),
        )
        for r in (1, 2, 3)
    ]

    for copy in ins_z:
        copy.wait_recv()
    own_span = pl.ds(pl.multiple_of(x * span, 16), span)
    ins_x = [
        send(in_rows.at[own_span], in_rows.at[own_span], in_send.at[3 + r], in_recv.at[3 + r], along_x(r))
        for r in (1, 2, 3)
    ]

    total = part[0:rows, :]
    for r in (1, 2, 3):
        partials[r - 1].wait_recv()
        total = total + partial_in[r - 1].astype(F32)
    branch[...] = total.astype(BF16)
    branches = send(branch, branch_in, relay_send.at[1], relay_recv.at[1], before)

    for copy in stat:
        copy.wait_recv()
    total = stats[z].astype(F32)
    for r in (1, 2, 3):
        total = total + stats_in[r - 1].astype(F32)
    count = jnp.sum(total[at_count:, :], axis=0, keepdims=True)
    in_factor[...] = total[at_gram:at_count, :] / count
    count = count[:, 0:1]
    for b in range(blocks):
        full = total[b * packed:b * packed + size, :] / count
        corner = total[b * packed + size:(b + 1) * packed, 0:size - head] / count
        out_factor[b, :, 0:head] = full
        out_factor[b, head:, head:] = corner
        out_factor[b, 0:head, head:] = full[head:, :].T
        weight = total[at_weight + b * size:at_weight + (b + 1) * size, :] / jnp.sqrt(count)
        left = jnp.dot(out_inverse[b], weight, precision=lax.Precision.HIGHEST, preferred_element_type=F32)
        precond[b * size:(b + 1) * size, :] = jnp.dot(
            left, in_inverse[...], precision=lax.Precision.HIGHEST, preferred_element_type=F32
        )

    for copy in ins_x:
        copy.wait_recv()
    relay.wait_recv()
    branches.wait_recv()
    tile = 512
    scale = jnp.where(section == sections - 1, 0.0, 1.0).astype(F32)
    for c in range(width // tile):
        columns = slice(c * tile, (c + 1) * tile)
        sums = relayed[:, columns].astype(F32) + nt_dot(branch_in[...], in_rows[columns, :])
        passed[:, columns] = (sums * scale).astype(BF16)

    for copy in outs + vals + [ins, relay, branches] + ins_z + ins_x + partials + stat + [splits[r] for r in (1, 2, 3)]:
        copy.wait_send()


def local(upstream, inputs, in_proj, out_proj, in_inverse, out_inverse, lengths):
    _, batches, slots, width = upstream.shape
    rows = batches * slots
    head = inputs.shape[3]
    shard = in_proj.shape[1]
    blocks, size = out_inverse.shape[1:3]
    span = RING * shard
    stat_rows = blocks * (2 * size - head) + shard + head + 16
    vmem = pl.BlockSpec(memory_space=pltpu.VMEM)
    dma = pltpu.SemaphoreType.DMA
    outs = pl.pallas_call(
        kernel,
        out_shape=(
            jax.ShapeDtypeStruct((rows, width), BF16),
            jax.ShapeDtypeStruct((shard, head), F32),
            jax.ShapeDtypeStruct((head, head), F32),
            jax.ShapeDtypeStruct((blocks, size, size), F32),
        ),
        in_specs=[pl.BlockSpec(memory_space=pltpu.SMEM)] + [vmem] * 6,
        out_specs=(vmem,) * 4,
        scratch_shapes=[
            pltpu.VMEM((rows, width), BF16),
            pltpu.VMEM((RING * rows, span), BF16),
            pltpu.VMEM((span, RING * rows), BF16),
            pltpu.VMEM((rows, width), BF16),
            pltpu.VMEM((RING, rows + 16, head), BF16),
            pltpu.VMEM((span, head), BF16),
            pltpu.VMEM((width, head), BF16),
            pltpu.VMEM((RING * rows, head), BF16),
            pltpu.VMEM((RING - 1, rows, head), BF16),
            pltpu.VMEM((rows, head), BF16),
            pltpu.VMEM((rows, head), BF16),
            pltpu.VMEM((RING, stat_rows, head), BF16),
            pltpu.VMEM((RING - 1, stat_rows, head), BF16),
            dma((3,)), dma((3,)), dma((3,)), dma((3,)), dma((3,)), dma((3,)),
            dma((2,)), dma((2,)), dma((7,)), dma((7,)), dma((3,)), dma((3,)), dma((3,)), dma((3,)),
        ],
        compiler_params=pltpu.CompilerParams(
            collective_id=0, has_side_effects=True, vmem_limit_bytes=48 * 1024 * 1024
        ),
    )(
        lengths.reshape(batches),
        upstream.reshape(rows, width),
        inputs.reshape(rows, head),
        in_proj[0],
        out_proj[0],
        in_inverse[0],
        out_inverse[0],
    )
    passed, precond, in_factor, out_factor = outs
    return (passed.reshape(upstream.shape), precond[None], in_factor[None], out_factor[None])


def solution(mesh):
    in_specs = (
        P("section", None, "dp", None),
        P("section", None, "dp", None),
        P("section", "dp", None),
        P("section", "dp", None),
        P("section", None, None),
        P("section", "dp", None, None),
        P("section", "dp", None),
    )
    out_specs = (
        P("section", None, "dp", None),
        P("section", "dp", None),
        P("section", None, None),
        P("section", "dp", None, None),
    )
    return jax.shard_map(local, mesh=mesh, in_specs=in_specs, out_specs=out_specs, check_vma=False)
```

time: 454 us -> 92.8 us (0.20)
  the two profiles are of different devices: /device:TPU:1 before, /device:TPU:80 now
where the time goes in v1:
time: 92.8 us; the launch traced here: 92.5 us
  Pallas kernels  81.9 us (88%)
  local copies, waits for them, and re-layouts  9.91 us (11%)
    pallas_call x1, Pallas kernels, local(): pl.pallas_call(kernel, out_shape=(jax.ShapeDtypeStruct((rows, width), BF1...  81.9 us
    unnamed x18, local copies, waits for them, and re-layouts  9.91 us

profile of v1, /device:TPU:80, one launch (start us, length us, event | category | flops | bytes accessed | tf_op | source)
XLA Modules:
  0.0 92.5 jit_solution(8329850554241315116)
XLA Ops:
  0.6 0.0 copy-start
  0.6 1.5 %copy-done = bf16[1,3,48,6656]{3,2,1,0:T(8,128)(2,1)S(1)} copy-done((bf16[1,3,48,6656]{3,2,1,0:T(8,128)(2,1)S(1)}, bf16[1,3,48,6656]{3,2,1,0:T(8,128)(2,1)}, u32[]{:S(2)}) %copy-start) | copy-done | bytes 1916952
  2.2 0.0 copy-start.1
  2.2 1.0 %copy-done.1 = f32[1,2,208,208]{3,2,1,0:T(8,128)S(1)} copy-done((f32[1,2,208,208]{3,2,1,0:T(8,128)S(1)}, f32[1,2,208,208]{3,2,1,0:T(8,128)}, u32[]{:S(2)}) %copy-start.1) | copy-done | bytes 346136
  3.2 0.0 copy-start.2
  3.2 0.9 copy-done.2
  4.1 0.0 copy-start.3
  4.1 0.9 copy-done.3
  5.0 0.0 copy-start.4
  5.0 0.8 copy-done.4
  5.8 0.0 copy-start.5
  5.8 0.8 copy-done.5
  6.6 0.0 copy-start.6
  6.6 0.7 copy-done.6
  7.2 81.9 %shard_map.102 = (bf16[144,6656]{1,0:T(8,128)(2,1)S(1)}, f32[416,128]{1,0:T(8,128)S(1)}, f32[128,128]{1,0:T(8,128)S(1)}, f32[2,208,208]{2,1,0:T(8,128)S(1)}) custom-call(s32[3]{0:T(128)S(1)} %bitcast.21, bf16[144,6656]{1,0:T(8,128)(2,1)S(1)} %bitcast.11, bf16[144,128]{1,0:T(8,128)(2,1)S(1)} %bitcast.20, bf16[416,128]{1,0:T(8,128)(2,1)S(1)} %bitcast.16, ...), custom_call_target="tpu_custom_call" | custom-call | tf_op jit(solution)/shard_map/pallas_call | solution.py:209
  89.2 1.3 %copy.15 = bf16[1,3,48,6656]{3,2,1,0:T(8,128)(2,1)} copy(bf16[1,3,48,6656]{3,2,1,0:T(8,128)(2,1)S(1)} %bitcast.12) | data formatting | bytes 3833856
  90.4 0.7 copy.16
  91.1 0.6 copy.17
  91.7 0.8 copy.18
Async XLA Ops:
  0.6 1.5 %copy-start = (bf16[1,3,48,6656]{3,2,1,0:T(8,128)(2,1)S(1)}, bf16[1,3,48,6656]{3,2,1,0:T(8,128)(2,1)}, u32[]{:S(2)}) copy-start(bf16[1,3,48,6656]{3,2,1,0:T(8,128)(2,1)} %param.7) | copy-start | bytes 5750788
  2.2 1.0 %copy-start.1 = (f32[1,2,208,208]{3,2,1,0:T(8,128)S(1)}, f32[1,2,208,208]{3,2,1,0:T(8,128)}, u32[]{:S(2)}) copy-start(f32[1,2,208,208]{3,2,1,0:T(8,128)} %param.12) | copy-start | bytes 1038340
  3.2 0.9 copy-start.2
  4.1 0.9 copy-start.3
  5.0 0.8 copy-start.4
  5.8 0.8 copy-start.5
  6.6 0.7 copy-start.6

commit v2 on v1

v2 whole, which is shorter than its diff:
```python
import jax
import jax.numpy as jnp
from jax import lax
from jax.experimental import pallas as pl
from jax.experimental.pallas import tpu as pltpu
from jax.sharding import PartitionSpec as P

RING = 4
BF16 = jnp.bfloat16
F32 = jnp.float32
MESH = pl.DeviceIdType.MESH
VMEM_LIMIT = 56 * 1024 * 1024


def nt_dot(a, b):
    return lax.dot_general(a, b, (((1,), (1,)), ((), ())), preferred_element_type=F32)


def tn_dot(a, b):
    return lax.dot_general(a, b, (((0,), (0,)), ((), ())), preferred_element_type=F32)


def grid_of(shape):
    return lax.broadcasted_iota(jnp.int32, shape, 0), lax.broadcasted_iota(jnp.int32, shape, 1)


def pack_pair(first, second):
    row, column = grid_of(first.shape)
    return jnp.where(column > row, first, second)


def diagonal(matrix):
    row, column = grid_of(matrix.shape)
    return jnp.sum(jnp.where(column == row, matrix, 0.0), axis=0, keepdims=True)


def unpack_pair(packed, diagonal_row):
    row, column = grid_of(packed.shape)
    flipped = packed.T
    first = jnp.where(column > row, packed, jnp.where(column < row, flipped, diagonal_row))
    second = jnp.where(column > row, flipped, packed)
    return first, second


def kernel(
    lengths_hbm, upstream, inputs, in_proj, out_proj, in_inverse_hbm, out_inverse_hbm,
    passed_hbm, precond_hbm, in_factor_hbm, out_factor_hbm,
    passed, precond, in_factor, out_factor, lengths, raw, raw_values, in_inverse, out_inverse,
    sent, split, split_t, relayed, values, out_rows, in_rows, partial, partial_in, branch, branch_in,
    own_gram, gram_in, quarter, quarter_in, stats, half_in, stats_in,
    load, drain, split_send, split_recv, value_send, value_recv, out_send, out_recv,
    relay_send, relay_recv, in_send, in_recv, partial_send, partial_recv, gram_send, gram_recv,
    quarter_send, quarter_recv, stats_send, stats_recv,
):
    rows, width = upstream.shape
    slots = rows // lengths.shape[0]
    shard, head = in_proj.shape
    blocks, size, _ = out_inverse.shape
    span = RING * shard
    edge = size - head
    sections = lax.axis_size("section")
    dp = lax.axis_index("dp")
    section = lax.axis_index("section")
    x = lax.div(dp, RING)
    z = lax.rem(dp, RING)
    before = {"section": lax.rem(section + sections - 1, sections)}
    after = {"section": lax.rem(section + 1, sections)}

    def along_x(r):
        return {"dp": lax.rem(x + r, RING) * RING + z}

    def along_z(r):
        return {"dp": x * RING + lax.rem(z + r, RING)}

    started = []

    def send(src, dst, send_sem, recv_sem, device):
        copy = pltpu.make_async_remote_copy(
            src_ref=src, dst_ref=dst, send_sem=send_sem, recv_sem=recv_sem, device_id=device, device_id_type=MESH
        )
        copy.start()
        started.append(copy)
        return copy

    def fetch(src, dst, sem):
        copy = pltpu.make_async_copy(src, dst, sem)
        copy.start()
        return copy

    def span_at(r):
        return pl.ds(pl.multiple_of(lax.rem(x + r, RING) * span, head), span)

    def shard_at(device_x, device_z):
        return pl.ds(pl.multiple_of((device_x * RING + device_z) * shard, 16), shard)

    def half_shard(device_x, device_z, which):
        return pl.ds(pl.multiple_of((device_x * RING + device_z) * shard + which * (shard // 2), 16), shard // 2)

    barrier = pltpu.get_barrier_semaphore()
    for device in [along_x(r) for r in (1, 2, 3)] + [along_z(r) for r in (1, 2, 3)] + [before, after]:
        pl.semaphore_signal(barrier, inc=1, device_id=device, device_id_type=MESH)

    own_out = pl.ds(pl.multiple_of(z * shard, 16), shard)
    loads = [fetch(lengths_hbm, lengths, load.at[0]), fetch(inputs, raw_values, load.at[1])]
    spans = {r: fetch(upstream.at[:, span_at(r)], raw.at[r], load.at[2 + r]) for r in (2, 1, 3, 0)}
    own_rows = fetch(out_proj, out_rows.at[own_out], load.at[6])
    inverses = [fetch(in_inverse_hbm, in_inverse, load.at[7]), fetch(out_inverse_hbm, out_inverse, load.at[8])]

    for copy in loads:
        copy.wait()
    position = lax.broadcasted_iota(jnp.int32, (rows, 1), 0)
    batch = lax.div(position, slots)
    limit = jnp.where(batch == 0, lengths[0], jnp.where(batch == 1, lengths[1], lengths[2]))
    keep = (lax.rem(position, slots) < limit).astype(F32)
    keep = jnp.broadcast_to(keep, (rows, head)).astype(BF16)
    counted = (lengths[0] + lengths[1] + lengths[2]).astype(F32)
    values[0, 0:rows, :] = raw_values[...] * keep
    values[0, rows:, :] = jnp.full((16, head), counted, F32).astype(BF16)
    shared = (RING + 1) * head
    pair = 2 * head
    tile_at = [3 * p for p in range(RING + 1)] + [3 * k + 1 + j for k in range(RING) for j in range(2)]

    def mask(r):
        spans[r].wait()
        for p, tile in enumerate(tile_at):
            masked = raw[r, :, tile * head:(tile + 1) * head] * keep
            sent[r, :, p * head:(p + 1) * head] = masked
            if r == 0:
                split[0:rows, p * head:(p + 1) * head] = masked

    mask(2)

    pl.semaphore_wait(barrier, 8)

    out_a = send(out_proj, out_rows.at[own_out], out_send.at[0], out_recv.at[0], along_z(1))
    out_b = send(out_proj, out_rows.at[own_out], out_send.at[1], out_recv.at[1], along_z(3))
    own_in = shard_at(x, z)
    in_first = send(in_proj, in_rows.at[own_in], in_send.at[0], in_recv.at[0], before)

    vals = [send(values.at[0], values.at[r], value_send.at[r - 1], value_recv.at[r - 1], along_x(r)) for r in (1, 2, 3)]

    def pair_at(step):
        return pl.ds(pl.multiple_of(shared + lax.rem(z + step, RING) * pair, head), pair)

    def scatter(step, r):
        where = pl.ds(0, shared) if step is None else pair_at(step)
        at = 0 if step is None else step + 1
        return send(
            sent.at[r, :, where], split.at[pl.ds(r * rows, rows), where],
            split_send.at[at, r - 1], split_recv.at[at, r - 1], along_x(r),
        )

    splits = {}
    for r in (2, 1, 3):
        if r != 2:
            mask(r)
        splits[None, r] = scatter(None, r)
    for r in (2, 1, 3):
        splits[2, r] = scatter(2, r)
    mask(0)
    for step in (1, 3, 0):
        for r in (2, 1, 3):
            splits[step, r] = scatter(step, r)

    def arrived(step):
        for r in (1, 3, 2):
            splits[step, r].wait_recv()

    cuts = ((0, shared), (shared, 2 * pair), (shared + 2 * pair, 2 * pair))
    relays = {}

    def relay(*pieces):
        for piece in pieces:
            r, cut = (0, 3, 1, 2)[piece // 3], piece % 3
            where = pl.ds(*cuts[cut])
            relays[r, cut] = send(
                sent.at[r, :, where], relayed.at[r, :, where], relay_send.at[piece], relay_recv.at[piece], before
            )

    in_first.wait_recv()
    in_a = send(in_rows.at[own_in], in_rows.at[own_in], in_send.at[1], in_recv.at[1], along_z(1))
    in_b = send(in_rows.at[own_in], in_rows.at[own_in], in_send.at[2], in_recv.at[2], along_z(3))
    left, right = lax.rem(z + 3, RING), lax.rem(z + 1, RING)
    half = shard // 2
    low = pl.ds(pl.multiple_of(left * shard, 16), half)
    high = pl.ds(pl.multiple_of(right * shard + half, 16), half)
    out_a.wait_recv()
    out_c = send(out_rows.at[low], out_rows.at[low], out_send.at[2], out_recv.at[2], along_z(1))
    out_b.wait_recv()
    out_d = send(out_rows.at[high], out_rows.at[high], out_send.at[3], out_recv.at[3], along_z(3))

    for copy in vals:
        copy.wait_recv()
    stacked = jnp.concatenate([values[r, 0:rows, :] for r in range(RING)], axis=0)
    quart = head // RING
    own_gram[...] = tn_dot(stacked, stacked).astype(BF16)
    gram_in[0, 0:quart, :] = own_gram[pl.ds(pl.multiple_of(x * quart, 16), quart), :]
    count_row = lax.broadcasted_iota(jnp.int32, (16, head), 0)
    counts = jnp.zeros((16, head), F32)
    for r in range(RING):
        counts = jnp.where(count_row == r, values[r, rows:, :].astype(F32), counts)
    gram_in[0, quart:, :] = counts.astype(BF16)
    grams = [send(gram_in.at[0], gram_in.at[r], gram_send.at[r - 1], gram_recv.at[r - 1], along_z(r)) for r in (1, 2, 3)]

    in_a.wait_recv()
    low_in = half_shard(x, left, 0)
    in_c = send(in_rows.at[low_in], in_rows.at[low_in], in_send.at[3], in_recv.at[3], along_z(1))
    in_b.wait_recv()
    high_in = half_shard(x, right, 1)
    in_d = send(in_rows.at[high_in], in_rows.at[high_in], in_send.at[4], in_recv.at[4], along_z(3))

    for copy in grams:
        copy.wait_recv()
    total = gram_in[0].astype(F32)
    for r in (1, 2, 3):
        total = total + gram_in[r].astype(F32)
    count = jnp.sum(total[quart:, :], axis=0, keepdims=True)
    quarter[...] = total[0:quart, :] / count
    count = count[:, 0:1]
    quarters = [
        send(quarter, quarter_in.at[r - 1], quarter_send.at[r - 1], quarter_recv.at[r - 1], along_x(r)) for r in (1, 2, 3)
    ]

    arrived(None)
    for p in range(RING + 1):
        split_t[3 * p * head:(3 * p + 1) * head, :] = split[:, p * head:(p + 1) * head].T

    def turn(step):
        first = (3 * lax.rem(z + step, RING) + 1) * head
        split_t[pl.ds(pl.multiple_of(first, head), pair), :] = split[:, pair_at(step)].T

    at_edge = head
    at_corner = at_edge + blocks * edge
    at_diagonal = at_corner + edge
    at_weight = at_diagonal + 16
    diagonal_row = lax.broadcasted_iota(jnp.int32, (16, head), 0)

    def statistics(r):
        owner = lax.rem(z + r, RING) * shard
        grams = []
        for b in range(blocks):
            g = split_t[pl.ds(pl.multiple_of(owner + b * size, 16), size), :]
            grams.append(nt_dot(g, g))
            stats[r, at_edge + b * edge:at_edge + (b + 1) * edge, :] = grams[b][head:, 0:head].astype(BF16)
        stats[r, 0:head, :] = pack_pair(grams[0][0:head, 0:head], grams[1][0:head, 0:head]).astype(BF16)
        corner = pack_pair(grams[0][head:, head:], grams[1][head:, head:])
        stats[r, at_corner:at_diagonal, 0:edge] = corner.astype(BF16)
        first = diagonal(grams[0][0:head, 0:head])
        stats[r, at_diagonal:at_weight, :] = jnp.where(diagonal_row == 0, first, 0.0).astype(BF16)
        second = diagonal(grams[0][head:, head:])
        stats[r, at_diagonal:at_weight, 0:edge] = jnp.where(
            diagonal_row[:, 0:edge] == 0, first[:, 0:edge], jnp.where(diagonal_row[:, 0:edge] == 1, second, 0.0)
        ).astype(BF16)
        weight = jnp.dot(
            split_t[pl.ds(pl.multiple_of(owner, 16), shard), :], stacked, preferred_element_type=F32
        )
        stats[r, at_weight:, :] = weight.astype(BF16)

    stat_rows = stats.shape[1]
    cut = stat_rows // 2
    top, bottom = pl.ds(0, cut), pl.ds(cut, cut)
    arrived(2)
    turn(2)
    statistics(2)
    half_a = send(stats.at[2, top], half_in.at[0], stats_send.at[0], stats_recv.at[0], along_z(1))
    half_b = send(stats.at[2, bottom], half_in.at[1], stats_send.at[1], stats_recv.at[1], along_z(3))
    arrived(1)
    turn(1)
    statistics(1)
    near_b = send(stats.at[1, bottom], stats_in.at[0, bottom], stats_send.at[2], stats_recv.at[2], along_z(1))
    arrived(3)
    turn(3)
    statistics(3)
    near_a = send(stats.at[3, top], stats_in.at[1, top], stats_send.at[3], stats_recv.at[3], along_z(3))
    half_a.wait_recv()
    stats[1, top, :] = (stats[1, top, :].astype(F32) + half_in[0].astype(F32)).astype(BF16)
    far_a = send(stats.at[1, top], stats_in.at[0, top], stats_send.at[4], stats_recv.at[4], along_z(1))
    half_b.wait_recv()
    stats[3, bottom, :] = (stats[3, bottom, :].astype(F32) + half_in[1].astype(F32)).astype(BF16)
    far_b = send(stats.at[3, bottom], stats_in.at[1, bottom], stats_send.at[5], stats_recv.at[5], along_z(3))

    arrived(0)
    own_rows.wait()
    out_c.wait_recv()
    out_d.wait_recv()
    ordered = [out_rows[3 * p * head:(3 * p + 1) * head, :] for p in range(RING + 1)]
    ordered += [out_rows[(3 * k + 1) * head:(3 * k + 3) * head, :] for k in range(RING)]
    part = jnp.dot(split[...], jnp.concatenate(ordered, axis=0), preferred_element_type=F32)
    partial[...] = part.astype(BF16)
    partials = [
        send(
            partial.at[pl.ds(r * rows, rows)], partial_in.at[r - 1],
            partial_send.at[r - 1], partial_recv.at[r - 1], along_x(RING - r),
        )
        for r in (1, 2, 3)
    ]

    in_c.wait_recv()
    in_d.wait_recv()
    own_span = pl.ds(pl.multiple_of(x * span, 16), span)
    in_x = [
        send(in_rows.at[own_span], in_rows.at[own_span], in_send.at[4 + r], in_recv.at[4 + r], along_x(r))
        for r in (1, 3, 2)
    ]

    turn(0)
    statistics(0)
    total = part[0:rows, :]
    for r in (1, 2, 3):
        partials[r - 1].wait_recv()
        total = total + partial_in[r - 1].astype(F32)
    branch[...] = total.astype(BF16)
    branches = send(branch, branch_in, relay_send.at[12], relay_recv.at[12], before)
    relay(*range(12))

    in_factor[pl.ds(pl.multiple_of(x * quart, 16), quart), :] = quarter[...]
    for r in (1, 2, 3):
        quarters[r - 1].wait_recv()
        source = lax.rem(x + RING - r, RING)
        in_factor[pl.ds(pl.multiple_of(source * quart, 16), quart), :] = quarter_in[r - 1]
    drained = [fetch(in_factor, in_factor_hbm, drain.at[0])]

    for copy in (near_a, near_b, far_a, far_b):
        copy.wait_recv()
    for copy in inverses:
        copy.wait()
    total = stats[0].astype(F32) + stats_in[0].astype(F32) + stats_in[1].astype(F32)
    heads = unpack_pair(total[0:head, :], total[at_diagonal:at_diagonal + 1, :])
    corners = unpack_pair(total[at_corner:at_diagonal, 0:edge], total[at_diagonal + 1:at_diagonal + 2, 0:edge])
    for b in range(blocks):
        side = total[at_edge + b * edge:at_edge + (b + 1) * edge, :] / count
        out_factor[b, 0:head, 0:head] = heads[b] / count
        out_factor[b, head:, 0:head] = side
        out_factor[b, 0:head, head:] = side.T
        out_factor[b, head:, head:] = corners[b] / count
        weight = total[at_weight + b * size:at_weight + (b + 1) * size, :] / jnp.sqrt(count)
        left_product = jnp.dot(out_inverse[b], weight, precision=lax.Precision.HIGHEST, preferred_element_type=F32)
        precond[b * size:(b + 1) * size, :] = jnp.dot(
            left_product, in_inverse[...], precision=lax.Precision.HIGHEST, preferred_element_type=F32
        )

    drained += [fetch(precond, precond_hbm, drain.at[1]), fetch(out_factor, out_factor_hbm, drain.at[2])]

    branches.wait_recv()
    scale = jnp.where(section == sections - 1, 0.0, 1.0).astype(F32)
    for copy, r in zip([None] + in_x, (0, 3, 1, 2)):
        if copy is not None:
            copy.wait_recv()
        first = lax.rem(x + r, RING) * span
        for cut, (start, extent) in enumerate(cuts):
            relays[r, cut].wait_recv()
            step = head if cut == 0 else pair
            for at in range(start, start + extent, step):
                columns = pl.ds(pl.multiple_of(first + tile_at[at // head] * head, head), step)
                sums = relayed[r, :, at:at + step].astype(F32) + nt_dot(branch_in[...], in_rows[columns, :])
                passed[:, columns] = (sums * scale).astype(BF16)
        drained.append(fetch(passed.at[:, span_at(r)], passed_hbm.at[:, span_at(r)], drain.at[3 + r]))

    for copy in started:
        copy.wait_send()
    for copy in drained:
        copy.wait()


def store(*refs):
    sources, targets, held, arrive, leave = refs[:4], refs[4:8], refs[8:12], refs[12], refs[13]
    width = sources[0].shape[1]
    piece = width // 4
    views = [lambda ref, i=i: ref.at[:, pl.ds(i * piece, piece)] for i in range(4)]
    parts = [(view(sources[0]), view(held[0]), view(targets[0])) for view in views]
    parts += list(zip(sources[1:], held[1:], targets[1:]))
    loads = [pltpu.make_async_copy(part[0], part[1], arrive.at[i]) for i, part in enumerate(parts)]
    stores = [pltpu.make_async_copy(part[1], part[2], leave.at[i]) for i, part in enumerate(parts)]
    for copy in loads:
        copy.start()
    for load, copy in zip(loads, stores):
        load.wait()
        copy.start()
    for copy in stores:
        copy.wait()


def local(upstream, inputs, in_proj, out_proj, in_inverse, out_inverse, lengths):
    _, batches, slots, width = upstream.shape
    rows = batches * slots
    head = inputs.shape[3]
    shard = in_proj.shape[1]
    blocks, size = out_inverse.shape[1:3]
    span = RING * shard
    edge = size - head
    stat_rows = head + blocks * edge + edge + 16 + shard
    hbm = pl.BlockSpec(memory_space=pltpu.HBM)
    dma = pltpu.SemaphoreType.DMA
    shapes = (
        jax.ShapeDtypeStruct((rows, width), BF16),
        jax.ShapeDtypeStruct((shard, head), F32),
        jax.ShapeDtypeStruct((head, head), F32),
        jax.ShapeDtypeStruct((blocks, size, size), F32),
    )
    outs = pl.pallas_call(
        kernel,
        out_shape=shapes,
        in_specs=[hbm] * 7,
        out_specs=(hbm,) * 4,
        scratch_shapes=[
            pltpu.VMEM((rows, width), BF16),
            pltpu.VMEM((shard, head), F32),
            pltpu.VMEM((head, head), F32),
            pltpu.VMEM((blocks, size, size), F32),
            pltpu.SMEM((batches,), jnp.int32),
            pltpu.VMEM((RING, rows, span), BF16),
            pltpu.VMEM((rows, head), BF16),
            pltpu.VMEM((head, head), F32),
            pltpu.VMEM((blocks, size, size), F32),
            pltpu.VMEM((RING, rows, span), BF16),
            pltpu.VMEM((RING * rows, span), BF16),
            pltpu.VMEM((span, RING * rows), BF16),
            pltpu.VMEM((RING, rows, span), BF16),
            pltpu.VMEM((RING, rows + 16, head), BF16),
            pltpu.VMEM((span, head), BF16),
            pltpu.VMEM((width, head), BF16),
            pltpu.VMEM((RING * rows, head), BF16),
            pltpu.VMEM((RING - 1, rows, head), BF16),
            pltpu.VMEM((rows, head), BF16),
            pltpu.VMEM((rows, head), BF16),
            pltpu.VMEM((head, head), BF16),
            pltpu.VMEM((RING, head // RING + 16, head), BF16),
            pltpu.VMEM((head // RING, head), F32),
            pltpu.VMEM((RING - 1, head // RING, head), F32),
            pltpu.VMEM((RING, stat_rows, head), BF16),
            pltpu.VMEM((2, stat_rows // 2, head), BF16),
            pltpu.VMEM((2, stat_rows, head), BF16),
            dma((9,)), dma((7,)), dma((5, 3)), dma((5, 3)), dma((3,)), dma((3,)), dma((4,)), dma((4,)),
            dma((13,)), dma((13,)), dma((8,)), dma((8,)), dma((3,)), dma((3,)), dma((3,)), dma((3,)),
            dma((3,)), dma((3,)), dma((6,)), dma((6,)),
        ],
        compiler_params=pltpu.CompilerParams(
            collective_id=0, has_side_effects=True, vmem_limit_bytes=VMEM_LIMIT
        ),
    )(
        lengths.reshape(batches),
        upstream.reshape(rows, width),
        inputs.reshape(rows, head),
        in_proj[0],
        out_proj[0],
        in_inverse[0],
        out_inverse[0],
    )
    passed, precond, in_factor, out_factor = pl.pallas_call(
        store,
        out_shape=shapes,
        in_specs=[hbm] * 4,
        out_specs=(hbm,) * 4,
        scratch_shapes=[pltpu.VMEM(shape.shape, shape.dtype) for shape in shapes] + [dma((7,)), dma((7,))],
        compiler_params=pltpu.CompilerParams(vmem_limit_bytes=VMEM_LIMIT),
    )(*outs)
    return (passed.reshape(upstream.shape), precond[None], in_factor[None], out_factor[None])


def solution(mesh):
    in_specs = (
        P("section", None, "dp", None),
        P("section", None, "dp", None),
        P("section", "dp", None),
        P("section", "dp", None),
        P("section", None, None),
        P("section", "dp", None, None),
        P("section", "dp", None),
    )
    out_specs = (
        P("section", None, "dp", None),
        P("section", "dp", None),
        P("section", None, None),
        P("section", "dp", None, None),
    )
    return jax.shard_map(local, mesh=mesh, in_specs=in_specs, out_specs=out_specs, check_vma=False)
```

time: 92.8 us -> 73.5 us (0.79)
  the two profiles are of different devices: /device:TPU:80 before, /device:TPU:1 now
where the time goes in v2:
time: 73.5 us; the launch traced here: 72.3 us
  Pallas kernels  71.7 us (98%)
    pallas_call x1, Pallas kernels, local(): pl.pallas_call(kernel, out_shape=shapes, in_specs=[hbm] * 7, out_specs=(h...  69.1 us
    pallas_call x1, Pallas kernels, local(): pl.pallas_call(store, out_shape=shapes, in_specs=[hbm] * 4, out_specs=(hb...  2.63 us

profile of v2, /device:TPU:1, one launch (start us, length us, event | category | flops | bytes accessed | tf_op | source)
XLA Modules:
  0.0 72.3 jit_solution(1341625170500741396)
XLA Ops:
  0.6 69.1 %shard_map.102 = (bf16[144,6656]{1,0:T(8,128)(2,1)}, f32[416,128]{1,0:T(8,128)}, f32[128,128]{1,0:T(8,128)}, f32[2,208,208]{2,1,0:T(8,128)}) custom-call(s32[3]{0:T(128)} %bitcast.17, bf16[144,6656]{1,0:T(8,128)(2,1)} %bitcast.11, bf16[144,128]{1,0:T(8,128)(2,1)} %bitcast.16, bf16[416,128]{1,0:T(8,128)(2,1)} %bitcast.13, bf16[416,128]{1,0:T(8,128)(2,1)} %bitcast.14, ...), custom_call_target="tpu_custom_call" | custom-call | tf_op jit(solution)/shard_map/pallas_call | solution.py:400
  69.7 2.6 %shard_map.103 = (bf16[144,6656]{1,0:T(8,128)(2,1)}, f32[416,128]{1,0:T(8,128)}, f32[128,128]{1,0:T(8,128)}, f32[2,208,208]{2,1,0:T(8,128)}) custom-call(bf16[144,6656]{1,0:T(8,128)(2,1)} %get-tuple-element.12.refs_0_, f32[416,128]{1,0:T(8,128)} %get-tuple-element.13.refs_1_, f32[128,128]{1,0:T(8,128)} %get-tuple-element.14.refs_2_, ...), custom_call_target="tpu_custom_call" | custom-call | tf_op jit(solution)/shard_map/pallas_call | solution.py:449

commit v3 on v2

--- a/solution.py
+++ b/solution.py
@@ -45,7 +45,7 @@
 def kernel(
     lengths_hbm, upstream, inputs, in_proj, out_proj, in_inverse_hbm, out_inverse_hbm,
     passed_hbm, precond_hbm, in_factor_hbm, out_factor_hbm,
-    passed, precond, in_factor, out_factor, lengths, raw, raw_values, in_inverse, out_inverse,
+    passed, precond, in_factor, out_factor, lengths, raw, raw_values, raw_proj, in_inverse, out_inverse,
     sent, split, split_t, relayed, values, out_rows, in_rows, partial, partial_in, branch, branch_in,
     own_gram, gram_in, quarter, quarter_in, stats, half_in, stats_in,
     load, drain, split_send, split_recv, value_send, value_recv, out_send, out_recv,
@@ -101,9 +101,10 @@
         pl.semaphore_signal(barrier, inc=1, device_id=device, device_id_type=MESH)
 
     own_out = pl.ds(pl.multiple_of(z * shard, 16), shard)
+    own_rows = fetch(out_proj, out_rows.at[own_out], load.at[6])
+    own_proj = fetch(in_proj, raw_proj, load.at[9])
     loads = [fetch(lengths_hbm, lengths, load.at[0]), fetch(inputs, raw_values, load.at[1])]
     spans = {r: fetch(upstream.at[:, span_at(r)], raw.at[r], load.at[2 + r]) for r in (2, 1, 3, 0)}
-    own_rows = fetch(out_proj, out_rows.at[own_out], load.at[6])
     inverses = [fetch(in_inverse_hbm, in_inverse, load.at[7]), fetch(out_inverse_hbm, out_inverse, load.at[8])]
 
     for copy in loads:
@@ -132,10 +133,12 @@
 
     pl.semaphore_wait(barrier, 8)
 
-    out_a = send(out_proj, out_rows.at[own_out], out_send.at[0], out_recv.at[0], along_z(1))
-    out_b = send(out_proj, out_rows.at[own_out], out_send.at[1], out_recv.at[1], along_z(3))
+    own_rows.wait()
+    own_proj.wait()
+    out_a = send(out_rows.at[own_out], out_rows.at[own_out], out_send.at[0], out_recv.at[0], along_z(1))
+    out_b = send(out_rows.at[own_out], out_rows.at[own_out], out_send.at[1], out_recv.at[1], along_z(3))
     own_in = shard_at(x, z)
-    in_first = send(in_proj, in_rows.at[own_in], in_send.at[0], in_recv.at[0], before)
+    in_first = send(raw_proj, in_rows.at[own_in], in_send.at[0], in_recv.at[0], before)
 
     vals = [send(values.at[0], values.at[r], value_send.at[r - 1], value_recv.at[r - 1], along_x(r)) for r in (1, 2, 3)]
 
@@ -272,21 +275,13 @@
     turn(3)
     statistics(3)
     near_a = send(stats.at[3, top], stats_in.at[1, top], stats_send.at[3], stats_recv.at[3], along_z(3))
-    half_a.wait_recv()
-    stats[1, top, :] = (stats[1, top, :].astype(F32) + half_in[0].astype(F32)).astype(BF16)
-    far_a = send(stats.at[1, top], stats_in.at[0, top], stats_send.at[4], stats_recv.at[4], along_z(1))
-    half_b.wait_recv()
-    stats[3, bottom, :] = (stats[3, bottom, :].astype(F32) + half_in[1].astype(F32)).astype(BF16)
-    far_b = send(stats.at[3, bottom], stats_in.at[1, bottom], stats_send.at[5], stats_recv.at[5], along_z(3))
-
     arrived(0)
-    own_rows.wait()
     out_c.wait_recv()
     out_d.wait_recv()
     ordered = [out_rows[3 * p * head:(3 * p + 1) * head, :] for p in range(RING + 1)]
     ordered += [out_rows[(3 * k + 1) * head:(3 * k + 3) * head, :] for k in range(RING)]
     part = jnp.dot(split[...], jnp.concatenate(ordered, axis=0), preferred_element_type=F32)
-    partial[...] = part.astype(BF16)
+    partial[...] = part
     partials = [
         send(
             partial.at[pl.ds(r * rows, rows)], partial_in.at[r - 1],
@@ -303,14 +298,23 @@
         for r in (1, 3, 2)
     ]
 
+    half_a.wait_recv()
+    stats[1, top, :] = (stats[1, top, :].astype(F32) + half_in[0].astype(F32)).astype(BF16)
+    far_a = send(stats.at[1, top], stats_in.at[0, top], stats_send.at[4], stats_recv.at[4], along_z(1))
+    half_b.wait_recv()
+    stats[3, bottom, :] = (stats[3, bottom, :].astype(F32) + half_in[1].astype(F32)).astype(BF16)
+    far_b = send(stats.at[3, bottom], stats_in.at[1, bottom], stats_send.at[5], stats_recv.at[5], along_z(3))
+
     turn(0)
     statistics(0)
     total = part[0:rows, :]
     for r in (1, 2, 3):
         partials[r - 1].wait_recv()
-        total = total + partial_in[r - 1].astype(F32)
+        total = total + partial_in[r - 1]
     branch[...] = total.astype(BF16)
     branches = send(branch, branch_in, relay_send.at[12], relay_recv.at[12], before)
+    near_a.wait_recv()
+    near_b.wait_recv()
     relay(*range(12))
 
     in_factor[pl.ds(pl.multiple_of(x * quart, 16), quart), :] = quarter[...]
@@ -320,7 +324,7 @@
         in_factor[pl.ds(pl.multiple_of(source * quart, 16), quart), :] = quarter_in[r - 1]
     drained = [fetch(in_factor, in_factor_hbm, drain.at[0])]
 
-    for copy in (near_a, near_b, far_a, far_b):
+    for copy in (far_a, far_b):
         copy.wait_recv()
     for copy in inverses:
         copy.wait()
@@ -410,6 +414,7 @@
             pltpu.SMEM((batches,), jnp.int32),
             pltpu.VMEM((RING, rows, span), BF16),
             pltpu.VMEM((rows, head), BF16),
+            pltpu.VMEM((shard, head), BF16),
             pltpu.VMEM((head, head), F32),
             pltpu.VMEM((blocks, size, size), F32),
             pltpu.VMEM((RING, rows, span), BF16),
@@ -419,8 +424,8 @@
             pltpu.VMEM((RING, rows + 16, head), BF16),
             pltpu.VMEM((span, head), BF16),
             pltpu.VMEM((width, head), BF16),
-            pltpu.VMEM((RING * rows, head), BF16),
-            pltpu.VMEM((RING - 1, rows, head), BF16),
+            pltpu.VMEM((RING * rows, head), F32),
+            pltpu.VMEM((RING - 1, rows, head), F32),
             pltpu.VMEM((rows, head), BF16),
             pltpu.VMEM((rows, head), BF16),
             pltpu.VMEM((head, head), BF16),
@@ -430,7 +435,7 @@
             pltpu.VMEM((RING, stat_rows, head), BF16),
             pltpu.VMEM((2, stat_rows // 2, head), BF16),
             pltpu.VMEM((2, stat_rows, head), BF16),
-            dma((9,)), dma((7,)), dma((5, 3)), dma((5, 3)), dma((3,)), dma((3,)), dma((4,)), dma((4,)),
+            dma((10,)), dma((7,)), dma((5, 3)), dma((5, 3)), dma((3,)), dma((3,)), dma((4,)), dma((4,)),
             dma((13,)), dma((13,)), dma((8,)), dma((8,)), dma((3,)), dma((3,)), dma((3,)), dma((3,)),
             dma((3,)), dma((3,)), dma((6,)), dma((6,)),
         ],

time: 73.5 us -> 72.5 us (0.986); the launches traced: 72.3 us -> 72.3 us
  no operation moved by 1% of the time
where the time goes in v3:
time: 72.5 us; the launch traced here: 72.3 us
  Pallas kernels  71.7 us (99%)
    pallas_call x1, Pallas kernels, local(): pl.pallas_call(kernel, out_shape=shapes, in_specs=[hbm] * 7, out_specs=(h...  69 us
    pallas_call x1, Pallas kernels, local(): pl.pallas_call(store, out_shape=shapes, in_specs=[hbm] * 4, out_specs=(hb...  2.63 us

profile of v3, /device:TPU:1, one launch (start us, length us, event | category | flops | bytes accessed | tf_op | source)
XLA Modules:
  0.0 72.3 jit_solution(8914093779767978212)
XLA Ops:
  0.6 69.0 %shard_map.102 = (bf16[144,6656]{1,0:T(8,128)(2,1)}, f32[416,128]{1,0:T(8,128)}, f32[128,128]{1,0:T(8,128)}, f32[2,208,208]{2,1,0:T(8,128)}) custom-call(s32[3]{0:T(128)} %bitcast.17, bf16[144,6656]{1,0:T(8,128)(2,1)} %bitcast.11, bf16[144,128]{1,0:T(8,128)(2,1)} %bitcast.16, bf16[416,128]{1,0:T(8,128)(2,1)} %bitcast.13, bf16[416,128]{1,0:T(8,128)(2,1)} %bitcast.14, ...), custom_call_target="tpu_custom_call" | custom-call | tf_op jit(solution)/shard_map/pallas_call | solution.py:404
  69.7 2.6 %shard_map.103 = (bf16[144,6656]{1,0:T(8,128)(2,1)}, f32[416,128]{1,0:T(8,128)}, f32[128,128]{1,0:T(8,128)}, f32[2,208,208]{2,1,0:T(8,128)}) custom-call(bf16[144,6656]{1,0:T(8,128)(2,1)} %get-tuple-element.12.refs_0_, f32[416,128]{1,0:T(8,128)} %get-tuple-element.13.refs_1_, f32[128,128]{1,0:T(8,128)} %get-tuple-element.14.refs_2_, ...), custom_call_target="tpu_custom_call" | custom-call | tf_op jit(solution)/shard_map/pallas_call | solution.py:454

commit v4 on v3

--- a/solution.py
+++ b/solution.py
@@ -172,13 +172,21 @@
     cuts = ((0, shared), (shared, 2 * pair), (shared + 2 * pair, 2 * pair))
     relays = {}
 
-    def relay(*pieces):
-        for piece in pieces:
-            r, cut = (0, 3, 1, 2)[piece // 3], piece % 3
-            where = pl.ds(*cuts[cut])
-            relays[r, cut] = send(
-                sent.at[r, :, where], relayed.at[r, :, where], relay_send.at[piece], relay_recv.at[piece], before
-            )
+    for piece in range(12):
+        r, cut = (0, 3, 1, 2)[piece // 3], piece % 3
+        where = pl.ds(*cuts[cut])
+        relays[r, cut] = pltpu.make_async_remote_copy(
+            src_ref=sent.at[r, :, where], dst_ref=relayed.at[r, :, where], send_sem=relay_send.at[piece],
+            recv_sem=relay_recv.at[piece], device_id=before, device_id_type=MESH,
+        )
+    started += relays.values()
+    same_chip = lax.rem(section, 2)
+
+    def relay(parity):
+        @pl.when(same_chip == parity)
+        def _():
+            for copy in relays.values():
+                copy.start()
 
     in_first.wait_recv()
     in_a = send(in_rows.at[own_in], in_rows.at[own_in], in_send.at[1], in_recv.at[1], along_z(1))
@@ -211,18 +219,6 @@
     in_b.wait_recv()
     high_in = half_shard(x, right, 1)
     in_d = send(in_rows.at[high_in], in_rows.at[high_in], in_send.at[4], in_recv.at[4], along_z(3))
-
-    for copy in grams:
-        copy.wait_recv()
-    total = gram_in[0].astype(F32)
-    for r in (1, 2, 3):
-        total = total + gram_in[r].astype(F32)
-    count = jnp.sum(total[quart:, :], axis=0, keepdims=True)
-    quarter[...] = total[0:quart, :] / count
-    count = count[:, 0:1]
-    quarters = [
-        send(quarter, quarter_in.at[r - 1], quarter_send.at[r - 1], quarter_recv.at[r - 1], along_x(r)) for r in (1, 2, 3)
-    ]
 
     arrived(None)
     for p in range(RING + 1):
@@ -267,6 +263,18 @@
     statistics(2)
     half_a = send(stats.at[2, top], half_in.at[0], stats_send.at[0], stats_recv.at[0], along_z(1))
     half_b = send(stats.at[2, bottom], half_in.at[1], stats_send.at[1], stats_recv.at[1], along_z(3))
+    for copy in grams:
+        copy.wait_recv()
+    total = gram_in[0].astype(F32)
+    for r in (1, 2, 3):
+        total = total + gram_in[r].astype(F32)
+    count = jnp.sum(total[quart:, :], axis=0, keepdims=True)
+    quarter[...] = total[0:quart, :] / count
+    count = count[:, 0:1]
+    quarters = [
+        send(quarter, quarter_in.at[r - 1], quarter_send.at[r - 1], quarter_recv.at[r - 1], along_x(r)) for r in (1, 2, 3)
+    ]
+
     arrived(1)
     turn(1)
     statistics(1)
@@ -315,7 +323,7 @@
     branches = send(branch, branch_in, relay_send.at[12], relay_recv.at[12], before)
     near_a.wait_recv()
     near_b.wait_recv()
-    relay(*range(12))
+    relay(0)
 
     in_factor[pl.ds(pl.multiple_of(x * quart, 16), quart), :] = quarter[...]
     for r in (1, 2, 3):
@@ -326,6 +334,7 @@
 
     for copy in (far_a, far_b):
         copy.wait_recv()
+    relay(1)
     for copy in inverses:
         copy.wait()
     total = stats[0].astype(F32) + stats_in[0].astype(F32) + stats_in[1].astype(F32)

time: 72.5 us -> 72.1 us (level)
  no operation moved by 1% of the time
where the time goes in v4:
time: 72.1 us; the launch traced here: 71.9 us
  Pallas kernels  71.3 us (99%)
    pallas_call x1, Pallas kernels, local(): pl.pallas_call(kernel, out_shape=shapes, in_specs=[hbm] * 7, out_specs=(h...  68.7 us
    pallas_call x1, Pallas kernels, local(): pl.pallas_call(store, out_shape=shapes, in_specs=[hbm] * 4, out_specs=(hb...  2.63 us

profile of v4, /device:TPU:1, one launch (start us, length us, event | category | flops | bytes accessed | tf_op | source)
XLA Modules:
  0.0 71.9 jit_solution(1006480315920185982)
XLA Ops:
  0.6 68.7 %shard_map.102 = (bf16[144,6656]{1,0:T(8,128)(2,1)}, f32[416,128]{1,0:T(8,128)}, f32[128,128]{1,0:T(8,128)}, f32[2,208,208]{2,1,0:T(8,128)}) custom-call(s32[3]{0:T(128)} %bitcast.17, bf16[144,6656]{1,0:T(8,128)(2,1)} %bitcast.11, bf16[144,128]{1,0:T(8,128)(2,1)} %bitcast.16, bf16[416,128]{1,0:T(8,128)(2,1)} %bitcast.13, bf16[416,128]{1,0:T(8,128)(2,1)} %bitcast.14, ...), custom_call_target="tpu_custom_call" | custom-call | tf_op jit(solution)/shard_map/pallas_call | solution.py:413
  69.3 2.6 %shard_map.103 = (bf16[144,6656]{1,0:T(8,128)(2,1)}, f32[416,128]{1,0:T(8,128)}, f32[128,128]{1,0:T(8,128)}, f32[2,208,208]{2,1,0:T(8,128)}) custom-call(bf16[144,6656]{1,0:T(8,128)(2,1)} %get-tuple-element.12.refs_0_, f32[416,128]{1,0:T(8,128)} %get-tuple-element.13.refs_1_, f32[128,128]{1,0:T(8,128)} %get-tuple-element.14.refs_2_, ...), custom_call_target="tpu_custom_call" | custom-call | tf_op jit(solution)/shard_map/pallas_call | solution.py:463
